TPU v7x, 512 devices: a whole 4x8x8 slice. The times are simulated.
512 devices in a mesh: ctx: 32 (over z, y_lo), ch: 16 (over x, y_hi, core).
Axes of the slice: x: 4, y: 8 (y_hi: 2, y_lo: 4; y = y_hi * 4 + y_lo), z: 8, core: 2. Of those that a mesh axis runs over, the one named last changes fastest.
Arguments:
- gate_stream: bfloat16 [8192, 4096], P('ctx', 'ch'), may hold values from -6 to 6
- key_stream: bfloat16 [8192, 4096], P('ctx', 'ch'), may hold values from -4 to 4
- value_stream: bfloat16 [8192, 4096], P('ctx', 'ch'), may hold values from -4 to 4
- filters: float32 [8192, 4096], P('ctx', 'ch'), may hold values from -4 to 4
- skip_gain: float32 [4096], P('ch'), may hold values from -3 to 3
- out_weight: bfloat16 [4096, 4096], P('ch'), may hold values from -0.125 to 0.125
Outputs:
- block_out: bfloat16 [8192, 4096], P('ctx', 'ch')
All inputs are finite; a program needn't handle non-finite values.
Results may differ from a plain program's by a relative error of at most 0.024.
Values may be sent and summed in bfloat16 or wider, within the bound.
A program may use at most 64 MiB of HBM per device.

v0:
```python
import math

import jax
import jax.numpy as jnp
from jax import lax
from jax.sharding import PartitionSpec as P

HIGH = lax.Precision.HIGHEST


def as_sent(x):
    return jax.tree.map(lambda a: a.astype(jnp.bfloat16) if a.dtype == jnp.float32 else a, x)


def angles(left, right, period):
    product = left[:, None] * right[None, :] % period
    return product.astype(jnp.float32) * (2.0 * math.pi / period)


def per_device(gate_stream, key_stream, value_stream, filters, skip_gain, out_weight):
    rows, width = value_stream.shape
    parts = lax.axis_size("ctx")
    place = lax.axis_index("ctx")
    span = rows // parts
    period = 2 * parts * rows
    mixed = key_stream.astype(jnp.float32) * value_stream.astype(jnp.float32)
    stacked = jnp.concatenate([mixed, filters], axis=1)[None]
    spread = lax.all_to_all(
        stacked.astype(jnp.bfloat16), "ctx", split_axis=1, concat_axis=0, tiled=True
    ).astype(stacked.dtype)
    block_ids = jnp.arange(parts, dtype=jnp.int32)
    freq_ids = jnp.arange(2 * parts, dtype=jnp.int32)
    outer = angles(freq_ids, block_ids, 2 * parts)
    first_real = jnp.einsum("kn,nmc->kmc", jnp.cos(outer), spread, precision=HIGH)
    first_imag = -jnp.einsum("kn,nmc->kmc", jnp.sin(outer), spread, precision=HIGH)
    inner_pos = place * span + jnp.arange(span, dtype=jnp.int32)
    twist = angles(freq_ids, inner_pos, period)
    twist_cos = jnp.cos(twist)[:, :, None]
    twist_sin = jnp.sin(twist)[:, :, None]
    turn_real = first_real * twist_cos + first_imag * twist_sin
    turn_imag = first_imag * twist_cos - first_real * twist_sin
    packed = jnp.concatenate([turn_real, turn_imag], axis=2)
    turned = lax.all_to_all(
        packed.astype(jnp.bfloat16), "ctx", split_axis=0, concat_axis=1, tiled=True
    ).astype(packed.dtype)
    part_real = turned[:, :, : 2 * width]
    part_imag = turned[:, :, 2 * width :]
    local_ids = jnp.arange(rows, dtype=jnp.int32)
    table = angles(local_ids, local_ids, rows)
    table_cos = jnp.cos(table)
    table_sin = jnp.sin(table)
    spec_real = jnp.einsum("kn,jnc->jkc", table_cos, part_real, precision=HIGH) + jnp.einsum(
        "kn,jnc->jkc", table_sin, part_imag, precision=HIGH
    )
    spec_imag = jnp.einsum("kn,jnc->jkc", table_cos, part_imag, precision=HIGH) - jnp.einsum(
        "kn,jnc->jkc", table_sin, part_real, precision=HIGH
    )
    sig_real = spec_real[:, :, :width]
    fil_real = spec_real[:, :, width:]
    sig_imag = spec_imag[:, :, :width]
    fil_imag = spec_imag[:, :, width:]
    prod_real = sig_real * fil_real - sig_imag * fil_imag
    prod_imag = sig_real * fil_imag + sig_imag * fil_real
    back_real = jnp.einsum("nk,jkc->jnc", table_cos, prod_real, precision=HIGH) - jnp.einsum(
        "nk,jkc->jnc", table_sin, prod_imag, precision=HIGH
    )
    back_imag = jnp.einsum("nk,jkc->jnc", table_cos, prod_imag, precision=HIGH) + jnp.einsum(
        "nk,jkc->jnc", table_sin, prod_real, precision=HIGH
    )
    own_freq = 2 * place + jnp.arange(2, dtype=jnp.int32)
    untwist = angles(own_freq, local_ids, period)
    untwist_cos = jnp.cos(untwist)[:, :, None]
    untwist_sin = jnp.sin(untwist)[:, :, None]
    done_real = back_real * untwist_cos - back_imag * untwist_sin
    done_imag = back_real * untwist_sin + back_imag * untwist_cos
    returned = lax.all_to_all(
        jnp.concatenate([done_real, done_imag], axis=2).astype(jnp.bfloat16),
        "ctx",
        split_axis=1,
        concat_axis=0,
        tiled=True,
    ).astype(jnp.float32)
    final_angle = angles(block_ids, freq_ids, 2 * parts)
    blocks_out = (
        jnp.einsum("nk,kmc->nmc", jnp.cos(final_angle), returned[:, :, :width], precision=HIGH)
        - jnp.einsum("nk,kmc->nmc", jnp.sin(final_angle), returned[:, :, width:], precision=HIGH)
    ) / period
    conv = lax.all_to_all(
        as_sent(blocks_out), "ctx", split_axis=0, concat_axis=1, tiled=True
    ).astype(blocks_out.dtype)[0]
    summed = conv + skip_gain[None, :] * mixed
    gated = (gate_stream.astype(jnp.float32) * summed).astype(jnp.bfloat16)
    flipped = lax.psum_scatter(
        lax.dot_general(
            out_weight, gated, (((0,), (1,)), ((), ())), preferred_element_type=jnp.float32
        ).astype(jnp.bfloat16),
        "ch",
        scatter_dimension=0,
        tiled=True,
    ).astype(jnp.float32)
    result = flipped.T
    return result.astype(jnp.bfloat16)


def solution(mesh):
    return jax.shard_map(
        per_device,
        mesh=mesh,
        in_specs=(
            P("ctx", "ch"),
            P("ctx", "ch"),
            P("ctx", "ch"),
            P("ctx", "ch"),
            P("ch"),
            P("ch", None),
        ),
        out_specs=P("ctx", "ch"),
        check_vma=False,
    )
```

profile of v0, /device:TPU:1, one launch (start us, length us, event | category | flops | bytes accessed | tf_op | source)
XLA Modules:
  0.0 224.8 jit_solution(6460434671585252050)
XLA Ops:
  6.5 0.0 copy-start
  6.5 1.3 fusion.38
  7.8 0.4 copy.54
  8.2 0.5 broadcast.230
  8.8 2.2 reduce
  11.0 0.8 reshape.164
  11.8 14.3 %all-to-all-start = ((bf16[32,2,2048]{2,1,0:T(2,128)(2,1)}), bf16[32,2,2048]{2,1,0:T(2,128)(2,1)S(1)}, u32[]{:S(2)}, u32[]{:S(2)}) async-start(bf16[32,2,2048]{2,1,0:T(2,128)(2,1)} %reshape.164), calls=%async_computation | async-start | bytes 524288 | tf_op jit(solution)/shard_map/all_to_all | solution.py:28
  26.1 0.1 fusion.86
  26.2 11.0 %all-to-all-done = bf16[32,2,2048]{2,1,0:T(2,128)(2,1)S(1)} async-done(((bf16[32,2,2048]{2,1,0:T(2,128)(2,1)}), bf16[32,2,2048]{2,1,0:T(2,128)(2,1)S(1)}, u32[]{:S(2)}, u32[]{:S(2)}) %all-to-all-start) | async-done | bytes 262176 | tf_op jit(solution)/shard_map/all_to_all | solution.py:28
  37.3 0.3 reshape.165
  37.6 0.7 fusion.36
  38.3 0.9 add_convert_fusion
  39.2 0.1 pad_maximum_fusion
  39.4 1.6 copy.30
  40.9 5.3 %all-to-all-start.1 = ((bf16[64,8,1024]{2,1,0:T(8,128)(2,1)}), bf16[64,8,1024]{2,1,0:T(8,128)(2,1)S(1)}, u32[]{:S(2)}, u32[]{:S(2)}) async-start(bf16[64,8,1024]{2,1,0:T(8,128)(2,1)} %copy.30), calls=%async_computation.1 | async-start | bytes 2097152 | tf_op jit(solution)/shard_map/all_to_all | solution.py:43
  46.2 0.2 reduce-scatter.2.cloned.1.call-start
  46.5 0.1 fusion.88
  46.6 25.9 %all-to-all-done.1 = bf16[64,8,1024]{2,1,0:T(8,128)(2,1)S(1)} async-done(((bf16[64,8,1024]{2,1,0:T(8,128)(2,1)}), bf16[64,8,1024]{2,1,0:T(8,128)(2,1)S(1)}, u32[]{:S(2)}, u32[]{:S(2)}) %all-to-all-start.1) | async-done | bytes 1048608 | tf_op jit(solution)/shard_map/all_to_all | solution.py:43
  72.5 0.1 copy.51
  72.6 1.6 fusion.8
  74.2 1.6 fusion.6
  75.9 1.7 fusion.2
  77.6 1.7 fusion.1
  79.3 0.1 multiply_subtract_fusion
  79.4 1.6 fusion.25
  81.0 1.6 fusion.27
  82.6 1.6 convolution_add_fusion.1
  84.1 1.9 fusion.14
  86.0 0.5 copy.34
  86.6 21.6 %all_to_all.57 = bf16[2,256,512]{2,0,1:T(2,128)(2,1)S(1)} all-to-all(bf16[2,256,512]{2,0,1:T(2,128)(2,1)S(1)} %copy.34), channel_id=1, replica_groups=mesh['ctx'=32,'ch'=16] {'ctx'}, dimensions={1} | all-to-all | bytes 1048576 | tf_op jit(solution)/shard_map/all_to_all | solution.py:76
  108.2 0.1 copy.52
  108.2 0.0 copy-start.1
  108.2 0.0 copy-start.2
  108.2 0.0 copy-start.3
  108.2 0.0 copy-start.4
  108.3 0.5 copy.36
  108.8 0.2 all_to_all.51
  109.0 0.3 fusion.17
  109.3 0.3 fusion.4
  109.7 0.1 copy.37
  109.8 16.8 %all_to_all.58 = bf16[32,8,256]{2,1,0:T(8,128)(2,1)S(1)} all-to-all(bf16[32,8,256]{2,1,0:T(8,128)(2,1)S(1)} %copy.37), channel_id=1, replica_groups=mesh['ctx'=32,'ch'=16] {'ctx'}, dimensions={0} | all-to-all | bytes 262144 | tf_op jit(solution)/shard_map/all_to_all | solution.py:88
  126.6 0.0 copy-done
  126.6 0.0 copy-done.1
  126.6 0.0 copy-done.2
  126.6 0.0 copy-done.3
  126.6 2.1 fusion
  128.6 0.0 reduce-scatter.2.cloned.1.call-update
  128.7 89.3 %reduce-scatter.2.cloned.1.call-done = bf16[256,256]{0,1:T(8,128)(2,1)} async-done(((bf16[4096,256]{0,1:T(8,128)(2,1)}), bf16[256,256]{0,1:T(8,128)(2,1)}) %reduce-scatter.2.cloned.1.call-update) | async-done | bytes 131088 | tf_op jit(solution)/shard_map/reduce_scatter | solution.py:93
  (6 shorter events, 0.1 us)
Async XLA Ops:
  6.5 120.0 %copy-start = (bf16[256,4096]{1,0:T(8,128)(2,1)S(1)}, bf16[256,4096]{1,0:T(8,128)(2,1)}, u32[]{:S(2)}) copy-start(bf16[256,4096]{1,0:T(8,128)(2,1)} %param.11) | copy-start | bytes 6291460
  11.8 25.5 %all-to-all-start = ((bf16[32,2,2048]{2,1,0:T(2,128)(2,1)}), bf16[32,2,2048]{2,1,0:T(2,128)(2,1)S(1)}, u32[]{:S(2)}, u32[]{:S(2)}) async-start(bf16[32,2,2048]{2,1,0:T(2,128)(2,1)} %reshape.164), calls=%async_computation | async-start | bytes 524288 | tf_op jit(solution)/shard_map/all_to_all | solution.py:28
  40.9 31.6 %all-to-all-start.1 = ((bf16[64,8,1024]{2,1,0:T(8,128)(2,1)}), bf16[64,8,1024]{2,1,0:T(8,128)(2,1)S(1)}, u32[]{:S(2)}, u32[]{:S(2)}) async-start(bf16[64,8,1024]{2,1,0:T(8,128)(2,1)} %copy.30), calls=%async_computation.1 | async-start | bytes 2097152 | tf_op jit(solution)/shard_map/all_to_all | solution.py:43
  46.2 171.8 %reduce-scatter.2.cloned.1.call-start = ((), (), s32[]{:S(2)}) async-start(), calls=%async_computation.5 | async-start | bytes 2228224 | tf_op jit(solution)/shard_map/reduce_scatter | solution.py:93
  108.2 18.4 %copy-start.1 = (bf16[256,256]{1,0:T(8,128)(2,1)S(1)}, bf16[256,256]{1,0:T(8,128)(2,1)}, u32[]{:S(2)}) copy-start(bf16[256,256]{1,0:T(8,128)(2,1)} %param.8) | copy-start | bytes 393220
  108.2 18.3 %copy-start.2 = (bf16[256,256]{1,0:T(8,128)(2,1)S(1)}, bf16[256,256]{1,0:T(8,128)(2,1)}, u32[]{:S(2)}) copy-start(bf16[256,256]{1,0:T(8,128)(2,1)} %param.7) | copy-start | bytes 393220
  108.2 18.3 %copy-start.3 = (bf16[256,256]{1,0:T(8,128)(2,1)S(1)}, bf16[256,256]{1,0:T(8,128)(2,1)}, u32[]{:S(2)}) copy-start(bf16[256,256]{1,0:T(8,128)(2,1)} %param.6) | copy-start | bytes 393220
  108.2 18.3 %copy-start.4 = (f32[256]{0:T(256)S(1)}, f32[256]{0:T(256)}, u32[]{:S(2)}) copy-start(f32[256]{0:T(256)} %param.10) | copy-start | bytes 3076
Sparse Core Ops, SparseCore 0:
  128.8 89.1 reduce-scatter.1
where the time goes:
time: 225 us
  waiting for transfers between devices  126 us (56%)
  blocking collectives  38.4 us (17%)
  starting transfers between devices  19.8 us (9%)
  matrix products  17.6 us (8%)
  between operations  13.7 us (6%)
  local copies, waits for them, and re-layouts  5.08 us (2%)
  other arithmetic  4.04 us (2%)
    reduce_scatter x1, waiting for transfers between devices, per_device(): lax.psum_scatter(lax.dot_general(out_weight, gated, (((0,), (1,)), ((), (...  89.3 us
    all_to_all x1, waiting for transfers between devices, per_device(): lax.all_to_all(packed.astype(jnp.bfloat16), 'ctx', split_axis=0, concat_a...  25.9 us
    all_to_all x1, blocking collectives, per_device(): lax.all_to_all(jnp.concatenate([done_real, done_imag], axis=2).astype(jnp...  21.6 us
    all_to_all x1, blocking collectives, per_device(): lax.all_to_all(as_sent(blocks_out), 'ctx', split_axis=0, concat_axis=1, t...  16.8 us
    all_to_all x1, starting transfers between devices, per_device(): lax.all_to_all(stacked.astype(jnp.bfloat16), 'ctx', split_axis=1, concat_...  14.3 us
    all_to_all x1, waiting for transfers between devices, per_device(): lax.all_to_all(stacked.astype(jnp.bfloat16), 'ctx', split_axis=1, concat_...  11 us
    all_to_all x1, starting transfers between devices, per_device(): lax.all_to_all(packed.astype(jnp.bfloat16), 'ctx', split_axis=0, concat_a...  5.3 us
  transfers between devices with their start and end apart: 3, of which 3 were waited for; matrix products, arithmetic and copies ran while one was open for 0% of the time, Pallas kernels for 0%

commit v1 on v0

v1 whole, which is shorter than its diff:
```python
import functools
import math

import jax
import jax.numpy as jnp
import numpy as np
from jax import lax
from jax.experimental import pallas as pl
from jax.experimental.pallas import tpu as pltpu
from jax.sharding import PartitionSpec as P

MESH = pl.DeviceIdType.MESH
F32 = jnp.float32
BF16 = jnp.bfloat16

CTX = 32
ROWS = 256
WIDTH = 256
OWN = WIDTH // CTX
NX = 4
TILE = 4


def tables():
    freq = np.arange(ROWS) + 0.5
    pos = np.arange(2 * ROWS)
    theta = 2.0 * math.pi * pos[:, None] * freq[None, :] / (2 * ROWS)
    forward = np.concatenate([np.cos(theta[:ROWS]), -np.sin(theta[:ROWS])], axis=1)
    backward = np.concatenate([np.cos(theta.T), -np.sin(theta.T)], axis=0) / ROWS
    return forward.astype(BF16), backward.astype(BF16)


def kernel(
    gate_hbm, key_hbm, value_hbm, filters_hbm, skip_hbm, weight_hbm, fwd_hbm, bwd_hbm,
    out_ref,
    gate, key, value, filters, skip, fwd, bwd,
    mixed, send1, recv1, sig, fil, prod, send2, recv2,
    gated, weight, part, got, ypart, ygot,
    in_sem, w_sem, wsend_sem, wrecv_sem, send_sem, recv_sem, gsend_sem, grecv_sem,
    xsend_sem, xrecv_sem, ysend_sem, yrecv_sem,
):
    c = lax.axis_index("ctx")
    h = lax.axis_index("ch")
    x = h // 4
    yhi = (h // 2) % 2
    core = h % 2
    sibling = (c, h + 1 - 2 * core)
    across = (c, h + 2 - 4 * yhi)

    def along_x(d):
        return (c, ((x + d) % NX) * 4 + yhi * 2 + core)

    loads = []
    for i, (src, dst) in enumerate(
        [(key_hbm, key), (value_hbm, value), (filters_hbm, filters), (fwd_hbm, fwd),
         (bwd_hbm, bwd), (gate_hbm, gate), (skip_hbm, skip)]
    ):
        load = pltpu.make_async_copy(src, dst, in_sem.at[i])
        load.start()
        loads.append(load)

    barrier = pltpu.get_barrier_semaphore()

    def greet(k, carry):
        pl.semaphore_signal(barrier, inc=1, device_id=((c + k) % CTX, h), device_id_type=MESH)
        return carry

    lax.fori_loop(1, CTX, greet, 0)
    others = [sibling, across] + [along_x(d) for d in range(1, NX)]
    for dev in others:
        pl.semaphore_signal(barrier, inc=1, device_id=dev, device_id_type=MESH)

    own_w = []
    for i in range(2 * NX):
        copy = pltpu.make_async_copy(
            weight_hbm.at[:, pl.ds(pl.multiple_of((2 * i + core) * WIDTH, WIDTH), WIDTH)],
            weight.at[i, pl.ds(0, WIDTH)],
            w_sem,
        )
        copy.start()

    loads[0].wait()
    loads[1].wait()
    mixed[...] = key[...].astype(F32) * value[...].astype(F32)
    loads[2].wait()
    mixed_t = mixed[...].T.reshape(CTX, OWN, ROWS)
    filters_t = filters[...].T.reshape(CTX, OWN, ROWS)
    send1[...] = jnp.concatenate([mixed_t, filters_t], axis=1).astype(BF16)
    recv1[c] = send1[c]

    pl.semaphore_wait(barrier, CTX - 1 + len(others))

    def scatter1(k, carry):
        to = (c + k) % CTX
        pltpu.make_async_remote_copy(
            src_ref=send1.at[to], dst_ref=recv1.at[c], send_sem=send_sem.at[0],
            recv_sem=recv_sem.at[0], device_id=(to, h), device_id_type=MESH,
        ).start()
        return carry

    lax.fori_loop(1, CTX, scatter1, 0)

    for i in range(2 * NX):
        pltpu.make_async_remote_copy(
            src_ref=weight_hbm.at[:, pl.ds(pl.multiple_of((2 * i + 1 - core) * WIDTH, WIDTH), WIDTH)],
            dst_ref=weight.at[i, pl.ds(WIDTH, WIDTH)],
            send_sem=wsend_sem, recv_sem=wrecv_sem, device_id=sibling, device_id_type=MESH,
        ).start()

    loads[3].wait()
    fil[:, 0:TILE] = jnp.zeros((3, TILE, OWN, ROWS), F32)
    wait1 = pltpu.make_async_remote_copy(
        src_ref=send1.at[pl.ds(0, CTX - 1)], dst_ref=recv1.at[pl.ds(0, CTX - 1)],
        send_sem=send_sem.at[0], recv_sem=recv_sem.at[0], device_id=sibling, device_id_type=MESH,
    )
    wait1.wait_recv()

    def transform(g, carry):
        block = recv1[pl.ds(8 * g, 8)].reshape(8 * 2 * OWN, ROWS)
        spec = jnp.dot(block, fwd[...], preferred_element_type=F32).reshape(8, 2 * OWN, 2 * ROWS)
        for ref, start, first in ((sig, 0, 0), (fil, TILE, OWN)):
            real = spec[:, first : first + OWN, :ROWS]
            imag = spec[:, first : first + OWN, ROWS:]
            ref[0, pl.ds(start + 8 * g, 8)] = real
            ref[1, pl.ds(start + 8 * g, 8)] = imag
            ref[2, pl.ds(start + 8 * g, 8)] = real + imag
        return carry

    lax.fori_loop(0, CTX // 8, transform, 0)

    for n in range(CTX // TILE):
        def step(t, sums):
            sums = list(sums)
            for p in range(3):
                for q in range(2):
                    lanes = slice(128 * q, 128 * q + 128)
                    left = [sig[p, TILE * t + j, :, lanes] for j in range(TILE)]
                    right = [
                        fil[p, TILE + TILE * (n - t) + d, :, lanes] for d in range(1 - TILE, TILE)
                    ]
                    for i in range(TILE):
                        at = (p * 2 + q) * TILE + i
                        for j in range(TILE):
                            sums[at] = sums[at] + left[j] * right[i - j + TILE - 1]
            return tuple(sums)

        zero = jnp.zeros((OWN, 128), F32)
        sums = lax.fori_loop(0, n + 1, step, (zero,) * (6 * TILE))
        for q in range(2):
            one, two, three = (
                jnp.concatenate(sums[(p * 2 + q) * TILE : (p * 2 + q + 1) * TILE], axis=0)
                for p in range(3)
            )
            rows = slice(TILE * OWN * n, TILE * OWN * (n + 1))
            prod[rows, 128 * q : 128 * q + 128] = (one - two).astype(BF16)
            prod[rows, ROWS + 128 * q : ROWS + 128 * q + 128] = (three - one - two).astype(BF16)

    loads[4].wait()
    back = jnp.dot(prod[...], bwd[...], preferred_element_type=F32).reshape(CTX, OWN, 2 * ROWS)
    tail = jnp.concatenate([jnp.zeros((1, OWN, ROWS), F32), back[:-1, :, ROWS:]], axis=0)
    conv = back[:, :, :ROWS] + tail
    send2[...] = jnp.concatenate([conv[:, :, :128], conv[:, :, 128:]], axis=1).astype(BF16)
    recv2[c] = send2[c]

    def scatter2(k, carry):
        to = (c + k) % CTX
        pltpu.make_async_remote_copy(
            src_ref=send2.at[to], dst_ref=recv2.at[c], send_sem=send_sem.at[1],
            recv_sem=recv_sem.at[1], device_id=(to, h), device_id_type=MESH,
        ).start()
        return carry

    lax.fori_loop(1, CTX, scatter2, 0)
    loads[5].wait()
    loads[6].wait()
    wait2 = pltpu.make_async_remote_copy(
        src_ref=send2.at[pl.ds(0, CTX - 1)], dst_ref=recv2.at[pl.ds(0, CTX - 1)],
        send_sem=send_sem.at[1], recv_sem=recv_sem.at[1], device_id=sibling, device_id_type=MESH,
    )
    wait2.wait_recv()

    back2 = recv2[...].astype(F32)
    for half in range(2):
        conv_t = back2[:, OWN * half : OWN * (half + 1), :].reshape(WIDTH, 128).T
        rows = slice(128 * half, 128 * half + 128)
        summed = conv_t + skip[...] * mixed[rows, :]
        gated[rows, 0:WIDTH] = (gate[rows, :].astype(F32) * summed).astype(BF16)

    share = pltpu.make_async_remote_copy(
        src_ref=gated.at[:, pl.ds(0, WIDTH)], dst_ref=gated.at[:, pl.ds(WIDTH, WIDTH)],
        send_sem=gsend_sem, recv_sem=grecv_sem, device_id=sibling, device_id_type=MESH,
    )
    share.start()
    pltpu.make_async_copy(weight.at[:, pl.ds(0, WIDTH)], weight.at[:, pl.ds(0, WIDTH)], w_sem).wait()
    waitw = pltpu.make_async_remote_copy(
        src_ref=weight.at[:, pl.ds(0, WIDTH)], dst_ref=weight.at[:, pl.ds(WIDTH, WIDTH)],
        send_sem=wsend_sem, recv_sem=wrecv_sem, device_id=sibling, device_id_type=MESH,
    )
    waitw.wait_recv()
    share.wait_recv()

    def block(d, y):
        return jnp.dot(
            gated[...], weight[((x + d) % NX) * 2 + y], preferred_element_type=F32
        )

    order = (2, 1, 3)
    xcopies = {}
    for s, y in enumerate((1 - yhi, yhi)):
        for k, d in enumerate(order):
            part[s, k] = block(d, y).astype(BF16)
            copy = pltpu.make_async_remote_copy(
                src_ref=part.at[s, k], dst_ref=got.at[s, k], send_sem=xsend_sem.at[s, k],
                recv_sem=xrecv_sem.at[s, k], device_id=along_x(d), device_id_type=MESH,
            )
            copy.start()
            xcopies[s, k] = copy

    total = block(0, 1 - yhi)
    for k in range(NX - 1):
        xcopies[0, k].wait_recv()
        total = total + got[0, k].astype(F32)
    ypart[...] = total.astype(BF16)
    ycopy = pltpu.make_async_remote_copy(
        src_ref=ypart, dst_ref=ygot, send_sem=ysend_sem, recv_sem=yrecv_sem,
        device_id=across, device_id_type=MESH,
    )
    ycopy.start()
    total = block(0, yhi)
    for k in range(NX - 1):
        xcopies[1, k].wait_recv()
        total = total + got[1, k].astype(F32)
    ycopy.wait_recv()
    out_ref[...] = (total + ygot[...].astype(F32)).astype(BF16)

    wait1.wait_send()
    wait2.wait_send()
    waitw.wait_send()
    share.wait_send()
    for copy in xcopies.values():
        copy.wait_send()
    ycopy.wait_send()


def per_device(gate_stream, key_stream, value_stream, filters, skip_gain, out_weight):
    fwd, bwd = tables()
    any_spec = pl.BlockSpec(memory_space=pl.ANY)
    dma = pltpu.SemaphoreType.DMA
    return pl.pallas_call(
        kernel,
        name="hyena",
        out_shape=jax.ShapeDtypeStruct((ROWS, WIDTH), BF16),
        in_specs=[any_spec] * 8,
        out_specs=pl.BlockSpec(memory_space=pltpu.VMEM),
        scratch_shapes=[
            pltpu.VMEM((ROWS, WIDTH), BF16),
            pltpu.VMEM((ROWS, WIDTH), BF16),
            pltpu.VMEM((ROWS, WIDTH), BF16),
            pltpu.VMEM((ROWS, WIDTH), F32),
            pltpu.VMEM((1, WIDTH), F32),
            pltpu.VMEM((ROWS, 2 * ROWS), BF16),
            pltpu.VMEM((2 * ROWS, 2 * ROWS), BF16),
            pltpu.VMEM((ROWS, WIDTH), F32),
            pltpu.VMEM((CTX, 2 * OWN, ROWS), BF16),
            pltpu.VMEM((CTX, 2 * OWN, ROWS), BF16),
            pltpu.VMEM((3, CTX, OWN, ROWS), F32),
            pltpu.VMEM((3, TILE + CTX, OWN, ROWS), F32),
            pltpu.VMEM((CTX * OWN, 2 * ROWS), BF16),
            pltpu.VMEM((CTX, 2 * OWN, 128), BF16),
            pltpu.VMEM((CTX, 2 * OWN, 128), BF16),
            pltpu.VMEM((ROWS, 2 * WIDTH), BF16),
            pltpu.VMEM((2 * NX, 2 * WIDTH, WIDTH), BF16),
            pltpu.VMEM((2, NX - 1, ROWS, WIDTH), BF16),
            pltpu.VMEM((2, NX - 1, ROWS, WIDTH), BF16),
            pltpu.VMEM((ROWS, WIDTH), BF16),
            pltpu.VMEM((ROWS, WIDTH), BF16),
            dma((7,)), dma, dma, dma, dma((2,)), dma((2,)), dma, dma,
            dma((2, NX - 1)), dma((2, NX - 1)), dma, dma,
        ],
        compiler_params=pltpu.CompilerParams(
            collective_id=0, has_side_effects=True, vmem_limit_bytes=48 << 20
        ),
    )(
        gate_stream, key_stream, value_stream, filters, skip_gain[None, :], out_weight,
        jnp.asarray(fwd), jnp.asarray(bwd),
    )


def solution(mesh):
    return jax.shard_map(
        per_device,
        mesh=mesh,
        in_specs=(
            P("ctx", "ch"),
            P("ctx", "ch"),
            P("ctx", "ch"),
            P("ctx", "ch"),
            P("ch"),
            P("ch", None),
        ),
        out_specs=P("ctx", "ch"),
        check_vma=False,
    )
```

time: 225 us -> 63.3 us (0.28)
  waiting for transfers between devices: 126 us -> 0 us
  Pallas kernels: 0 us -> 54.4 us
  blocking collectives: 38.4 us -> 0 us
  starting transfers between devices: 19.8 us -> 0 us
  matrix products: 17.6 us -> 0 us
  between operations: 13.7 us -> 0.02 us
  other arithmetic: 4.04 us -> 0 us
  local copies, waits for them, and re-layouts: 5.08 us -> 8.58 us
    reduce_scatter x1 -> x0, waiting for transfers between devices: 89.3 us -> none  [per_device(): lax.psum_scatter(lax.dot_general(out_weight, gated, (((0,), (1,)), ((), (...]
    pallas_call x0 -> x1, Pallas kernels: none -> 54.4 us  [per_device(): pl.pallas_call(kernel, name='hyena', out_shape=jax.ShapeDtypeStruct((ROWS...]
    all_to_all x2 -> x0, blocking collectives: 38.4 us -> none  [the longest x1 21.6 us: per_device(): lax.all_to_all(jnp.concatenate([done_real, done_imag], axis=2).astype(jnp...]
    all_to_all x2 -> x0, waiting for transfers between devices: 36.9 us -> none  [the longest x1 25.9 us: per_device(): lax.all_to_all(packed.astype(jnp.bfloat16), 'ctx', split_axis=0, concat_a...]
    all_to_all x2 -> x0, starting transfers between devices: 19.6 us -> none  [the longest x1 14.3 us: per_device(): lax.all_to_all(stacked.astype(jnp.bfloat16), 'ctx', split_axis=1, concat_...]
    dot_general x13 -> x0, matrix products: 17.6 us -> none  [the longest x1 2.06 us: per_device(): lax.dot_general(out_weight, gated, (((0,), (1,)), ((), ())), preferred_el...]
    unnamed x14 -> x17, local copies, waits for them, and re-layouts: 1.65 us -> 8.58 us
    concatenate x3 -> x0, local copies, waits for them, and re-layouts: 2.47 us -> none  [the longest x1 1.56 us: per_device(): packed = jnp.concatenate([turn_real, turn_imag], axis=2)]
  transfers between devices with their start and end apart: 3 -> 0, of which waited for: 3 -> 0; matrix products, arithmetic and copies ran while one was open for 0% -> 0% of each run, Pallas kernels for 0% -> 0%
where the time goes in v1:
time: 63.3 us; the launch traced here: 63 us
  Pallas kernels  54.4 us (86%)
  local copies, waits for them, and re-layouts  8.58 us (14%)
    pallas_call x1, Pallas kernels, per_device(): pl.pallas_call(kernel, name='hyena', out_shape=jax.ShapeDtypeStruct((ROWS...  54.4 us
    unnamed x17, local copies, waits for them, and re-layouts  8.58 us

profile of v1, /device:TPU:1, one launch (start us, length us, event | category | flops | bytes accessed | tf_op | source)
XLA Modules:
  0.0 63.0 jit_solution(8658349223825333417)
XLA Ops:
  0.0 0.0 copy-start
  0.0 1.6 %copy-done = bf16[256,4096]{1,0:T(8,128)(2,1)S(1)} copy-done((bf16[256,4096]{1,0:T(8,128)(2,1)S(1)}, bf16[256,4096]{1,0:T(8,128)(2,1)}, u32[]{:S(2)}) %copy-start) | copy-done | bytes 2097176
  1.6 0.0 copy-start.1
  1.6 1.0 %copy-done.1 = bf16[512,512]{1,0:T(8,128)(2,1)S(1)} copy-done((bf16[512,512]{1,0:T(8,128)(2,1)S(1)}, bf16[512,512]{1,0:T(8,128)(2,1)}, u32[]{:S(2)}) %copy-start.1) | copy-done | bytes 524312
  2.6 0.0 copy-start.2
  2.6 0.9 %copy-done.2 = f32[256,256]{1,0:T(8,128)S(1)} copy-done((f32[256,256]{1,0:T(8,128)S(1)}, f32[256,256]{1,0:T(8,128)}, u32[]{:S(2)}) %copy-start.2) | copy-done | bytes 262168
  3.6 0.0 copy-start.3
  3.6 0.9 %copy-done.3 = bf16[256,512]{1,0:T(8,128)(2,1)S(1)} copy-done((bf16[256,512]{1,0:T(8,128)(2,1)S(1)}, bf16[256,512]{1,0:T(8,128)(2,1)}, u32[]{:S(2)}) %copy-start.3) | copy-done | bytes 262168
  4.5 0.0 copy-start.4
  4.5 0.9 %copy-done.4 = bf16[256,256]{1,0:T(8,128)(2,1)S(1)} copy-done((bf16[256,256]{1,0:T(8,128)(2,1)S(1)}, bf16[256,256]{1,0:T(8,128)(2,1)}, u32[]{:S(2)}) %copy-start.4) | copy-done | bytes 131096
  5.4 0.0 copy-start.5
  5.4 0.9 %copy-done.5 = bf16[256,256]{1,0:T(8,128)(2,1)S(1)} copy-done((bf16[256,256]{1,0:T(8,128)(2,1)S(1)}, bf16[256,256]{1,0:T(8,128)(2,1)}, u32[]{:S(2)}) %copy-start.5) | copy-done | bytes 131096
  6.3 0.0 copy-start.6
  6.3 0.9 %copy-done.6 = bf16[256,256]{1,0:T(8,128)(2,1)S(1)} copy-done((bf16[256,256]{1,0:T(8,128)(2,1)S(1)}, bf16[256,256]{1,0:T(8,128)(2,1)}, u32[]{:S(2)}) %copy-start.6) | copy-done | bytes 131096
  7.2 0.0 copy-start.7
  7.3 0.7 %copy-done.7 = f32[256]{0:T(256)S(1)} copy-done((f32[256]{0:T(256)S(1)}, f32[256]{0:T(256)}, u32[]{:S(2)}) %copy-start.7) | copy-done | bytes 1048
  7.9 54.4 %hyena.1 = bf16[256,256]{1,0:T(8,128)(2,1)S(1)} custom-call(bf16[256,256]{1,0:T(8,128)(2,1)S(1)} %copy-done.4, bf16[256,256]{1,0:T(8,128)(2,1)S(1)} %copy-done.5, bf16[256,256]{1,0:T(8,128)(2,1)S(1)} %copy-done.6, f32[256,256]{1,0:T(8,128)S(1)} %copy-done.2, f32[1,256]{1,0:T(1,128)S(1)} %bitcast.1, bf16[256,4096]{1,0:T(8,128)(2,1)S(1)} %copy-done, ...), custom_call_target="tpu_custom_call" | custom-call | tf_op jit(solution)/shard_map/hyena/pallas_call | solution.py:249
  62.3 0.7 %copy.10 = bf16[256,256]{1,0:T(8,128)(2,1)} copy(bf16[256,256]{1,0:T(8,128)(2,1)S(1)} %hyena.1) | data formatting | bytes 262144
Async XLA Ops:
  0.0 1.6 %copy-start = (bf16[256,4096]{1,0:T(8,128)(2,1)S(1)}, bf16[256,4096]{1,0:T(8,128)(2,1)}, u32[]{:S(2)}) copy-start(bf16[256,4096]{1,0:T(8,128)(2,1)} %weight_hbm.1) | copy-start | bytes 6291460
  1.6 1.0 %copy-start.1 = (bf16[512,512]{1,0:T(8,128)(2,1)S(1)}, bf16[512,512]{1,0:T(8,128)(2,1)}, u32[]{:S(2)}) copy-start(bf16[512,512]{1,0:T(8,128)(2,1)} %constant.5.clone.bwd_hbm) | copy-start | bytes 1572868
  2.6 0.9 %copy-start.2 = (f32[256,256]{1,0:T(8,128)S(1)}, f32[256,256]{1,0:T(8,128)}, u32[]{:S(2)}) copy-start(f32[256,256]{1,0:T(8,128)} %filters_hbm.1) | copy-start | bytes 786436
  3.6 0.9 %copy-start.3 = (bf16[256,512]{1,0:T(8,128)(2,1)S(1)}, bf16[256,512]{1,0:T(8,128)(2,1)}, u32[]{:S(2)}) copy-start(bf16[256,512]{1,0:T(8,128)(2,1)} %constant.4.clone.fwd_hbm) | copy-start | bytes 786436
  4.5 0.9 %copy-start.4 = (bf16[256,256]{1,0:T(8,128)(2,1)S(1)}, bf16[256,256]{1,0:T(8,128)(2,1)}, u32[]{:S(2)}) copy-start(bf16[256,256]{1,0:T(8,128)(2,1)} %gate_hbm.1) | copy-start | bytes 393220
  5.4 0.9 %copy-start.5 = (bf16[256,256]{1,0:T(8,128)(2,1)S(1)}, bf16[256,256]{1,0:T(8,128)(2,1)}, u32[]{:S(2)}) copy-start(bf16[256,256]{1,0:T(8,128)(2,1)} %key_hbm.1) | copy-start | bytes 393220
  6.3 0.9 %copy-start.6 = (bf16[256,256]{1,0:T(8,128)(2,1)S(1)}, bf16[256,256]{1,0:T(8,128)(2,1)}, u32[]{:S(2)}) copy-start(bf16[256,256]{1,0:T(8,128)(2,1)} %value_hbm.1) | copy-start | bytes 393220
  7.2 0.7 %copy-start.7 = (f32[256]{0:T(256)S(1)}, f32[256]{0:T(256)}, u32[]{:S(2)}) copy-start(f32[256]{0:T(256)} %param.12) | copy-start | bytes 3076

commit v2 on v1

v2 whole, which is shorter than its diff:
```python
import functools
import math

import jax
import jax.numpy as jnp
import numpy as np
from jax import lax
from jax.experimental import pallas as pl
from jax.experimental.pallas import tpu as pltpu
from jax.sharding import PartitionSpec as P

MESH = pl.DeviceIdType.MESH
F32 = jnp.float32
BF16 = jnp.bfloat16

CTX = 32
ROWS = 256
WIDTH = 256
OWN = WIDTH // CTX
NX = 4
CHUNKS = 4
TILE = 4


def tables():
    freq = np.arange(ROWS) + 0.5
    pos = np.arange(2 * ROWS)
    theta = 2.0 * math.pi * pos[:, None] * freq[None, :] / (2 * ROWS)
    forward = np.concatenate([np.cos(theta[:ROWS]), -np.sin(theta[:ROWS])], axis=1)
    backward = np.concatenate([np.cos(theta.T), -np.sin(theta.T)], axis=0) / ROWS
    return forward.astype(BF16), backward.astype(BF16)


def kernel(
    gate_hbm, key_hbm, value_hbm, filters_hbm, skip_hbm, weight_hbm, fwd_hbm, bwd_hbm,
    out_ref,
    gate, key, value, filters, skip, fwd, bwd,
    mixed, send1, recv1, sig, fil, send2, recv2,
    gated, weight, part, got, own, ypart, ygot,
    in_sem, w_sem, wsend_sem, wrecv_sem, send_sem, recv_sem, recv2_sem, gsend_sem, grecv_sem,
    xsend_sem, xrecv_sem, ysend_sem, yrecv_sem,
):
    c = lax.axis_index("ctx")
    h = lax.axis_index("ch")
    x = h // 4
    yhi = (h // 2) % 2
    core = h % 2
    sibling = (c, h + 1 - 2 * core)
    across = (c, h + 2 - 4 * yhi)

    def along_x(d):
        return (c, ((x + d) % NX) * 4 + yhi * 2 + core)

    loads = []
    for i, (src, dst) in enumerate(
        [(key_hbm, key), (value_hbm, value), (filters_hbm, filters), (fwd_hbm, fwd),
         (bwd_hbm, bwd), (gate_hbm, gate), (skip_hbm, skip)]
    ):
        load = pltpu.make_async_copy(src, dst, in_sem.at[i])
        load.start()
        loads.append(load)

    barrier = pltpu.get_barrier_semaphore()

    def greet(k, carry):
        pl.semaphore_signal(barrier, inc=1, device_id=((c + k) % CTX, h), device_id_type=MESH)
        return carry

    lax.fori_loop(1, CTX, greet, 0, unroll=True)
    others = [sibling, across] + [along_x(d) for d in range(1, NX)]
    for dev in others:
        pl.semaphore_signal(barrier, inc=1, device_id=dev, device_id_type=MESH)

    for i in range(2 * NX):
        copy = pltpu.make_async_copy(
            weight_hbm.at[:, pl.ds(pl.multiple_of((2 * i + core) * WIDTH, WIDTH), WIDTH)],
            weight.at[i, pl.ds(0, WIDTH)],
            w_sem,
        )
        copy.start()

    loads[0].wait()
    loads[1].wait()
    mixed[...] = key[...].astype(F32) * value[...].astype(F32)
    loads[2].wait()
    mixed_t = mixed[...].T.reshape(CTX, OWN, ROWS)
    filters_t = filters[...].T.reshape(CTX, OWN, ROWS)
    send1[...] = jnp.concatenate([mixed_t, filters_t], axis=1).astype(BF16)
    pltpu.make_async_copy(send1.at[c], recv1.at[c], recv_sem.at[c // TILE]).start()

    pl.semaphore_wait(barrier, CTX - 1 + len(others))

    def scatter1(k, carry):
        to = (c + k) % CTX
        pltpu.make_async_remote_copy(
            src_ref=send1.at[to], dst_ref=recv1.at[c], send_sem=send_sem.at[0],
            recv_sem=recv_sem.at[c // TILE], device_id=(to, h), device_id_type=MESH,
        ).start()
        return carry

    lax.fori_loop(1, CTX, scatter1, 0, unroll=True)

    for i in range(2 * NX):
        pltpu.make_async_remote_copy(
            src_ref=weight_hbm.at[:, pl.ds(pl.multiple_of((2 * i + 1 - core) * WIDTH, WIDTH), WIDTH)],
            dst_ref=weight.at[i, pl.ds(WIDTH, WIDTH)],
            send_sem=wsend_sem, recv_sem=wrecv_sem, device_id=sibling, device_id_type=MESH,
        ).start()

    loads[3].wait()
    fil[:, 0:TILE] = jnp.zeros((3, TILE, OWN, ROWS), F32)
    last = jnp.zeros((1, OWN, ROWS), F32)
    for n in range(CTX // TILE):
        tile = pl.ds(TILE * n, TILE)
        pltpu.make_async_copy(send1.at[tile], recv1.at[tile], recv_sem.at[n]).wait()
        spec = jnp.dot(
            recv1[tile].reshape(TILE * 2 * OWN, ROWS), fwd[...], preferred_element_type=F32
        ).reshape(TILE, 2 * OWN, 2 * ROWS)
        for ref, start, low in ((sig, 0, 0), (fil, TILE, OWN)):
            real = spec[:, low : low + OWN, :ROWS]
            imag = spec[:, low : low + OWN, ROWS:]
            ref[0, pl.ds(start + TILE * n, TILE)] = real
            ref[1, pl.ds(start + TILE * n, TILE)] = imag
            ref[2, pl.ds(start + TILE * n, TILE)] = real + imag

        def step(t, sums):
            sums = list(sums)
            for p in range(3):
                for q in range(2):
                    lanes = slice(128 * q, 128 * q + 128)
                    left = [sig[p, TILE * t + j, :, lanes] for j in range(TILE)]
                    right = [
                        fil[p, TILE + TILE * (n - t) + d, :, lanes] for d in range(1 - TILE, TILE)
                    ]
                    for i in range(TILE):
                        at = (p * 2 + q) * TILE + i
                        for j in range(TILE):
                            sums[at] = sums[at] + left[j] * right[i - j + TILE - 1]
            return tuple(sums)

        zero = jnp.zeros((OWN, 128), F32)
        sums = lax.fori_loop(0, n + 1, step, (zero,) * (6 * TILE))
        one, two, three = (
            jnp.concatenate(
                [jnp.concatenate(sums[(2 * p + q) * TILE : (2 * p + q + 1) * TILE], axis=0) for q in range(2)],
                axis=1,
            )
            for p in range(3)
        )
        prod = jnp.concatenate([one - two, three - one - two], axis=1).astype(BF16)
        if n == 0:
            loads[4].wait()
        back = jnp.dot(prod, bwd[...], preferred_element_type=F32).reshape(TILE, OWN, 2 * ROWS)
        conv = back[:, :, :ROWS] + jnp.concatenate([last, back[:-1, :, ROWS:]], axis=0)
        last = back[TILE - 1 :, :, ROWS:]
        send2[tile] = jnp.concatenate([conv[:, :, :128], conv[:, :, 128:]], axis=1).astype(BF16)
        for to in range(TILE * n, TILE * (n + 1)):
            @pl.when(to != c)
            def _():
                pltpu.make_async_remote_copy(
                    src_ref=send2.at[to], dst_ref=recv2.at[c], send_sem=send_sem.at[1],
                    recv_sem=recv2_sem, device_id=(to, h), device_id_type=MESH,
                ).start()

            @pl.when(to == c)
            def _():
                pltpu.make_async_copy(send2.at[to], recv2.at[c], recv2_sem).start()

    loads[5].wait()
    loads[6].wait()
    pltpu.make_async_copy(send2, recv2, recv2_sem).wait()

    back2 = recv2[...].astype(F32)
    for half in range(2):
        conv_t = back2[:, OWN * half : OWN * (half + 1), :].reshape(WIDTH, 128).T
        rows = slice(128 * half, 128 * half + 128)
        summed = conv_t + skip[...] * mixed[rows, :]
        gated[rows, 0:WIDTH] = (gate[rows, :].astype(F32) * summed).astype(BF16)

    share = pltpu.make_async_remote_copy(
        src_ref=gated.at[:, pl.ds(0, WIDTH)], dst_ref=gated.at[:, pl.ds(WIDTH, WIDTH)],
        send_sem=gsend_sem, recv_sem=grecv_sem, device_id=sibling, device_id_type=MESH,
    )
    share.start()
    pltpu.make_async_copy(weight.at[:, pl.ds(0, WIDTH)], weight.at[:, pl.ds(0, WIDTH)], w_sem).wait()
    waitw = pltpu.make_async_remote_copy(
        src_ref=weight.at[:, pl.ds(0, WIDTH)], dst_ref=weight.at[:, pl.ds(WIDTH, WIDTH)],
        send_sem=wsend_sem, recv_sem=wrecv_sem, device_id=sibling, device_id_type=MESH,
    )
    waitw.wait_recv()
    share.wait_recv()

    def block(d, y, rows=slice(None)):
        return jnp.dot(
            gated[rows], weight[((x + d) % NX) * 2 + y], preferred_element_type=F32
        )

    order = (2, 1, 3)
    step = ROWS // CHUNKS

    def send_x(s, k, r, rows):
        copy = pltpu.make_async_remote_copy(
            src_ref=part.at[s, k, rows], dst_ref=got.at[s, k, rows], send_sem=xsend_sem.at[s, k, r],
            recv_sem=xrecv_sem.at[s, k, r], device_id=along_x(order[k]), device_id_type=MESH,
        )
        copy.start()
        return copy

    first = []
    for r in range(CHUNKS):
        rows = pl.ds(step * r, step)
        for k, d in enumerate(order):
            part[0, k, rows] = block(d, 1 - yhi, rows).astype(BF16)
        first.append([send_x(0, k, r, rows) for k in range(NX - 1)])
    second = []
    for k, d in enumerate(order):
        part[1, k] = block(d, yhi).astype(BF16)
        second.append(send_x(1, k, 0, pl.ds(0, ROWS)))
    own[0] = block(0, 1 - yhi)
    own[1] = block(0, yhi)
    ycopies = []
    for r in range(CHUNKS):
        rows = pl.ds(step * r, step)
        total = own[0, rows]
        for k in range(NX - 1):
            first[r][k].wait_recv()
            total = total + got[0, k, rows].astype(F32)
        ypart[rows] = total.astype(BF16)
        copy = pltpu.make_async_remote_copy(
            src_ref=ypart.at[rows], dst_ref=ygot.at[rows], send_sem=ysend_sem.at[r],
            recv_sem=yrecv_sem.at[r], device_id=across, device_id_type=MESH,
        )
        copy.start()
        ycopies.append(copy)
    total = own[1]
    for k in range(NX - 1):
        second[k].wait_recv()
        total = total + got[1, k].astype(F32)
    own[1] = total
    for r in range(CHUNKS):
        rows = pl.ds(step * r, step)
        ycopies[r].wait_recv()
        out_ref[rows] = (own[1, rows] + ygot[rows].astype(F32)).astype(BF16)

    for n, (sent, landed) in enumerate(((send1, recv1), (send2, recv2))):
        pltpu.make_async_remote_copy(
            src_ref=sent.at[pl.ds(0, CTX - 1)], dst_ref=landed.at[pl.ds(0, CTX - 1)],
            send_sem=send_sem.at[n], recv_sem=recv2_sem, device_id=sibling, device_id_type=MESH,
        ).wait_send()
    waitw.wait_send()
    share.wait_send()
    for copy in sum(first, []) + second + ycopies:
        copy.wait_send()


def per_device(gate_stream, key_stream, value_stream, filters, skip_gain, out_weight):
    fwd, bwd = tables()
    any_spec = pl.BlockSpec(memory_space=pl.ANY)
    dma = pltpu.SemaphoreType.DMA
    return pl.pallas_call(
        kernel,
        name="hyena",
        out_shape=pltpu.VMEM((ROWS, WIDTH), BF16),
        in_specs=[any_spec] * 8,
        out_specs=pl.BlockSpec(memory_space=pltpu.VMEM),
        scratch_shapes=[
            pltpu.VMEM((ROWS, WIDTH), BF16),
            pltpu.VMEM((ROWS, WIDTH), BF16),
            pltpu.VMEM((ROWS, WIDTH), BF16),
            pltpu.VMEM((ROWS, WIDTH), F32),
            pltpu.VMEM((1, WIDTH), F32),
            pltpu.VMEM((ROWS, 2 * ROWS), BF16),
            pltpu.VMEM((2 * ROWS, 2 * ROWS), BF16),
            pltpu.VMEM((ROWS, WIDTH), F32),
            pltpu.VMEM((CTX, 2 * OWN, ROWS), BF16),
            pltpu.VMEM((CTX, 2 * OWN, ROWS), BF16),
            pltpu.VMEM((3, CTX, OWN, ROWS), F32),
            pltpu.VMEM((3, TILE + CTX, OWN, ROWS), F32),
            pltpu.VMEM((CTX, 2 * OWN, 128), BF16),
            pltpu.VMEM((CTX, 2 * OWN, 128), BF16),
            pltpu.VMEM((ROWS, 2 * WIDTH), BF16),
            pltpu.VMEM((2 * NX, 2 * WIDTH, WIDTH), BF16),
            pltpu.VMEM((2, NX - 1, ROWS, WIDTH), BF16),
            pltpu.VMEM((2, NX - 1, ROWS, WIDTH), BF16),
            pltpu.VMEM((2, ROWS, WIDTH), F32),
            pltpu.VMEM((ROWS, WIDTH), BF16),
            pltpu.VMEM((ROWS, WIDTH), BF16),
            dma((7,)), dma, dma, dma, dma((2,)), dma((CTX // TILE,)), dma, dma, dma,
            dma((2, NX - 1, CHUNKS)), dma((2, NX - 1, CHUNKS)), dma((CHUNKS,)), dma((CHUNKS,)),
        ],
        compiler_params=pltpu.CompilerParams(
            collective_id=0, has_side_effects=True, vmem_limit_bytes=56 << 20
        ),
    )(
        gate_stream, key_stream, value_stream, filters, skip_gain[None, :], out_weight,
        jnp.asarray(fwd), jnp.asarray(bwd),
    )


def solution(mesh):
    return jax.shard_map(
        per_device,
        mesh=mesh,
        in_specs=(
            P("ctx", "ch"),
            P("ctx", "ch"),
            P("ctx", "ch"),
            P("ctx", "ch"),
            P("ch"),
            P("ch", None),
        ),
        out_specs=P("ctx", "ch"),
        check_vma=False,
    )
```

time: 63.3 us -> 47.6 us (0.75)
  local copies, waits for them, and re-layouts: 8.58 us -> 0.66 us
  Pallas kernels: 54.4 us -> 46.8 us
    unnamed x17 -> x1, local copies, waits for them, and re-layouts: 8.58 us -> 0.66 us
    pallas_call x1, Pallas kernels: 54.4 us -> 46.8 us  [per_device(): pl.pallas_call(kernel, name='hyena', out_shape=pltpu.VMEM((ROWS, WIDTH),...]
where the time goes in v2:
time: 47.6 us; the launch traced here: 47.5 us
  Pallas kernels  46.8 us (98%)
  local copies, waits for them, and re-layouts  0.66 us (1%)
    pallas_call x1, Pallas kernels, per_device(): pl.pallas_call(kernel, name='hyena', out_shape=pltpu.VMEM((ROWS, WIDTH),...  46.8 us

profile of v2, /device:TPU:1, one launch (start us, length us, event | category | flops | bytes accessed | tf_op | source)
XLA Modules:
  0.0 47.5 jit_solution(1594547616639884288)
XLA Ops:
  0.0 46.8 %hyena.1 = bf16[256,256]{1,0:T(8,128)(2,1)S(1)} custom-call(bf16[256,256]{1,0:T(8,128)(2,1)} %gate_hbm.1, bf16[256,256]{1,0:T(8,128)(2,1)} %key_hbm.1, bf16[256,256]{1,0:T(8,128)(2,1)} %value_hbm.1, f32[256,256]{1,0:T(8,128)} %filters_hbm.1, f32[1,256]{1,0:T(1,128)} %bitcast.1, bf16[256,4096]{1,0:T(8,128)(2,1)} %weight_hbm.1, ...), custom_call_target="tpu_custom_call" | custom-call | tf_op jit(solution)/shard_map/hyena/pallas_call | solution.py:260
  46.8 0.7 %copy.10 = bf16[256,256]{1,0:T(8,128)(2,1)} copy(bf16[256,256]{1,0:T(8,128)(2,1)S(1)} %hyena.1) | data formatting | bytes 262144

commit v3 on v2

--- a/solution.py
+++ b/solution.py
@@ -35,10 +35,10 @@
     gate_hbm, key_hbm, value_hbm, filters_hbm, skip_hbm, weight_hbm, fwd_hbm, bwd_hbm,
     out_ref,
     gate, key, value, filters, skip, fwd, bwd,
-    mixed, send1, recv1, sig, fil, send2, recv2,
-    gated, weight, part, got, own, ypart, ygot,
+    send1, recv1, sig, fil, send2, recv2,
+    gated, weight, part, got, ring, ringgot, onward, own, ypart, ygot,
     in_sem, w_sem, wsend_sem, wrecv_sem, send_sem, recv_sem, recv2_sem, gsend_sem, grecv_sem,
-    xsend_sem, xrecv_sem, ysend_sem, yrecv_sem,
+    xsend_sem, xrecv_sem, rsend_sem, rrecv_sem, ysend_sem, yrecv_sem,
 ):
     c = lax.axis_index("ctx")
     h = lax.axis_index("ch")
@@ -53,8 +53,8 @@
 
     loads = []
     for i, (src, dst) in enumerate(
-        [(key_hbm, key), (value_hbm, value), (filters_hbm, filters), (fwd_hbm, fwd),
-         (bwd_hbm, bwd), (gate_hbm, gate), (skip_hbm, skip)]
+        [(key_hbm, key.at[0]), (value_hbm, value.at[0]), (filters_hbm, filters), (fwd_hbm, fwd),
+         (bwd_hbm, bwd), (gate_hbm, gate.at[0]), (skip_hbm, skip.at[0])]
     ):
         load = pltpu.make_async_copy(src, dst, in_sem.at[i])
         load.start()
@@ -81,9 +81,9 @@
 
     loads[0].wait()
     loads[1].wait()
-    mixed[...] = key[...].astype(F32) * value[...].astype(F32)
+    mixed = key[0].astype(F32) * value[0].astype(F32)
     loads[2].wait()
-    mixed_t = mixed[...].T.reshape(CTX, OWN, ROWS)
+    mixed_t = mixed.T.reshape(CTX, OWN, ROWS)
     filters_t = filters[...].T.reshape(CTX, OWN, ROWS)
     send1[...] = jnp.concatenate([mixed_t, filters_t], axis=1).astype(BF16)
     pltpu.make_async_copy(send1.at[c], recv1.at[c], recv_sem.at[c // TILE]).start()
@@ -106,6 +106,17 @@
             dst_ref=weight.at[i, pl.ds(WIDTH, WIDTH)],
             send_sem=wsend_sem, recv_sem=wrecv_sem, device_id=sibling, device_id_type=MESH,
         ).start()
+    streams = [
+        pltpu.make_async_remote_copy(
+            src_ref=src, dst_ref=dst.at[1], send_sem=gsend_sem.at[i], recv_sem=grecv_sem.at[i],
+            device_id=sibling, device_id_type=MESH,
+        )
+        for i, (src, dst) in enumerate(
+            [(key_hbm, key), (value_hbm, value), (gate_hbm, gate), (skip_hbm, skip)]
+        )
+    ]
+    for copy in streams:
+        copy.start()
 
     loads[3].wait()
     fil[:, 0:TILE] = jnp.zeros((3, TILE, OWN, ROWS), F32)
@@ -158,37 +169,40 @@
             @pl.when(to != c)
             def _():
                 pltpu.make_async_remote_copy(
-                    src_ref=send2.at[to], dst_ref=recv2.at[c], send_sem=send_sem.at[1],
-                    recv_sem=recv2_sem, device_id=(to, h), device_id_type=MESH,
+                    src_ref=send2.at[to], dst_ref=recv2.at[0, c], send_sem=send_sem.at[1],
+                    recv_sem=recv2_sem.at[0], device_id=(to, h), device_id_type=MESH,
                 ).start()
 
             @pl.when(to == c)
             def _():
-                pltpu.make_async_copy(send2.at[to], recv2.at[c], recv2_sem).start()
+                pltpu.make_async_copy(send2.at[to], recv2.at[0, c], recv2_sem.at[0]).start()
+
+            pltpu.make_async_remote_copy(
+                src_ref=send2.at[to], dst_ref=recv2.at[1, c], send_sem=send_sem.at[2],
+                recv_sem=recv2_sem.at[1], device_id=(to, sibling[1]), device_id_type=MESH,
+            ).start()
+
 
     loads[5].wait()
     loads[6].wait()
-    pltpu.make_async_copy(send2, recv2, recv2_sem).wait()
-
-    back2 = recv2[...].astype(F32)
-    for half in range(2):
-        conv_t = back2[:, OWN * half : OWN * (half + 1), :].reshape(WIDTH, 128).T
-        rows = slice(128 * half, 128 * half + 128)
-        summed = conv_t + skip[...] * mixed[rows, :]
-        gated[rows, 0:WIDTH] = (gate[rows, :].astype(F32) * summed).astype(BF16)
-
-    share = pltpu.make_async_remote_copy(
-        src_ref=gated.at[:, pl.ds(0, WIDTH)], dst_ref=gated.at[:, pl.ds(WIDTH, WIDTH)],
-        send_sem=gsend_sem, recv_sem=grecv_sem, device_id=sibling, device_id_type=MESH,
-    )
-    share.start()
+    for copy in streams:
+        copy.wait_recv()
+    for s in range(2):
+        pltpu.make_async_copy(send2, recv2.at[s], recv2_sem.at[s]).wait()
+        returned = recv2[s].astype(F32)
+        for i in range(2):
+            rows = slice(128 * i, 128 * i + 128)
+            conv_t = returned[:, OWN * i : OWN * (i + 1), :].reshape(WIDTH, 128).T
+            mixed = key[s, rows].astype(F32) * value[s, rows].astype(F32)
+            summed = conv_t + skip[s] * mixed
+            gated[rows, WIDTH * s : WIDTH * (s + 1)] = (gate[s, rows].astype(F32) * summed).astype(BF16)
+
     pltpu.make_async_copy(weight.at[:, pl.ds(0, WIDTH)], weight.at[:, pl.ds(0, WIDTH)], w_sem).wait()
     waitw = pltpu.make_async_remote_copy(
         src_ref=weight.at[:, pl.ds(0, WIDTH)], dst_ref=weight.at[:, pl.ds(WIDTH, WIDTH)],
         send_sem=wsend_sem, recv_sem=wrecv_sem, device_id=sibling, device_id_type=MESH,
     )
     waitw.wait_recv()
-    share.wait_recv()
 
     def block(d, y, rows=slice(None)):
         return jnp.dot(
@@ -197,25 +211,42 @@
 
     order = (2, 1, 3)
     step = ROWS // CHUNKS
-
-    def send_x(s, k, r, rows):
+    half = ROWS // 2
+    top, bottom = slice(0, half), slice(half, ROWS)
+
+    def send_across(r):
+        rows = pl.ds(step * r, step)
+        copies = []
+        for k, d in enumerate(order):
+            part[k, rows] = block(d, 1 - yhi, rows).astype(BF16)
+            copy = pltpu.make_async_remote_copy(
+                src_ref=part.at[k, rows], dst_ref=got.at[k, rows], send_sem=xsend_sem.at[k, r],
+                recv_sem=xrecv_sem.at[k, r], device_id=along_x(d), device_id_type=MESH,
+            )
+            copy.start()
+            copies.append(copy)
+        return copies
+
+    def send_ring(i, terms):
+        ring[i] = terms.astype(BF16)
         copy = pltpu.make_async_remote_copy(
-            src_ref=part.at[s, k, rows], dst_ref=got.at[s, k, rows], send_sem=xsend_sem.at[s, k, r],
-            recv_sem=xrecv_sem.at[s, k, r], device_id=along_x(order[k]), device_id_type=MESH,
+            src_ref=ring.at[i], dst_ref=ringgot.at[i], send_sem=rsend_sem.at[i],
+            recv_sem=rrecv_sem.at[i], device_id=along_x(3 if i % 2 else 1), device_id_type=MESH,
         )
         copy.start()
         return copy
 
-    first = []
-    for r in range(CHUNKS):
-        rows = pl.ds(step * r, step)
-        for k, d in enumerate(order):
-            part[0, k, rows] = block(d, 1 - yhi, rows).astype(BF16)
-        first.append([send_x(0, k, r, rows) for k in range(NX - 1)])
-    second = []
-    for k, d in enumerate(order):
-        part[1, k] = block(d, yhi).astype(BF16)
-        second.append(send_x(1, k, 0, pl.ds(0, ROWS)))
+    def arrived(i):
+        ringcopies[i].wait_recv()
+        return ringgot[i].astype(F32)
+
+    first = [send_across(r) for r in range(CHUNKS)]
+    far = block(2, yhi)
+    ringcopies = [send_ring(0, far[top]), send_ring(1, far[bottom])]
+    right, left = block(1, yhi), block(3, yhi)
+    ringcopies += [send_ring(2, right[bottom]), send_ring(3, left[top])]
+    onward[0] = right[top]
+    onward[1] = left[bottom]
     own[0] = block(0, 1 - yhi)
     own[1] = block(0, yhi)
     ycopies = []
@@ -224,7 +255,7 @@
         total = own[0, rows]
         for k in range(NX - 1):
             first[r][k].wait_recv()
-            total = total + got[0, k, rows].astype(F32)
+            total = total + got[k, rows].astype(F32)
         ypart[rows] = total.astype(BF16)
         copy = pltpu.make_async_remote_copy(
             src_ref=ypart.at[rows], dst_ref=ygot.at[rows], send_sem=ysend_sem.at[r],
@@ -232,24 +263,22 @@
         )
         copy.start()
         ycopies.append(copy)
-    total = own[1]
-    for k in range(NX - 1):
-        second[k].wait_recv()
-        total = total + got[1, k].astype(F32)
-    own[1] = total
+    ringcopies += [send_ring(4 + i, onward[i] + arrived(i)) for i in range(2)]
+    own[1, top] = own[1, top] + arrived(3) + arrived(4)
+    own[1, bottom] = own[1, bottom] + arrived(2) + arrived(5)
     for r in range(CHUNKS):
         rows = pl.ds(step * r, step)
         ycopies[r].wait_recv()
         out_ref[rows] = (own[1, rows] + ygot[rows].astype(F32)).astype(BF16)
 
-    for n, (sent, landed) in enumerate(((send1, recv1), (send2, recv2))):
+    for n, count in enumerate((CTX - 1, CTX - 1, CTX)):
+        sent = (send1, send2, send2)[n].at[pl.ds(0, count)]
         pltpu.make_async_remote_copy(
-            src_ref=sent.at[pl.ds(0, CTX - 1)], dst_ref=landed.at[pl.ds(0, CTX - 1)],
-            send_sem=send_sem.at[n], recv_sem=recv2_sem, device_id=sibling, device_id_type=MESH,
+            src_ref=sent, dst_ref=sent, send_sem=send_sem.at[n], recv_sem=recv2_sem.at[0],
+            device_id=sibling, device_id_type=MESH,
         ).wait_send()
     waitw.wait_send()
-    share.wait_send()
-    for copy in sum(first, []) + second + ycopies:
+    for copy in streams + sum(first, []) + ringcopies + ycopies:
         copy.wait_send()
 
 
@@ -264,29 +293,31 @@
         in_specs=[any_spec] * 8,
         out_specs=pl.BlockSpec(memory_space=pltpu.VMEM),
         scratch_shapes=[
-            pltpu.VMEM((ROWS, WIDTH), BF16),
-            pltpu.VMEM((ROWS, WIDTH), BF16),
-            pltpu.VMEM((ROWS, WIDTH), BF16),
+            pltpu.VMEM((2, ROWS, WIDTH), BF16),
+            pltpu.VMEM((2, ROWS, WIDTH), BF16),
+            pltpu.VMEM((2, ROWS, WIDTH), BF16),
             pltpu.VMEM((ROWS, WIDTH), F32),
-            pltpu.VMEM((1, WIDTH), F32),
+            pltpu.VMEM((2, 1, WIDTH), F32),
             pltpu.VMEM((ROWS, 2 * ROWS), BF16),
             pltpu.VMEM((2 * ROWS, 2 * ROWS), BF16),
-            pltpu.VMEM((ROWS, WIDTH), F32),
             pltpu.VMEM((CTX, 2 * OWN, ROWS), BF16),
             pltpu.VMEM((CTX, 2 * OWN, ROWS), BF16),
             pltpu.VMEM((3, CTX, OWN, ROWS), F32),
             pltpu.VMEM((3, TILE + CTX, OWN, ROWS), F32),
             pltpu.VMEM((CTX, 2 * OWN, 128), BF16),
-            pltpu.VMEM((CTX, 2 * OWN, 128), BF16),
+            pltpu.VMEM((2, CTX, 2 * OWN, 128), BF16),
             pltpu.VMEM((ROWS, 2 * WIDTH), BF16),
             pltpu.VMEM((2 * NX, 2 * WIDTH, WIDTH), BF16),
-            pltpu.VMEM((2, NX - 1, ROWS, WIDTH), BF16),
-            pltpu.VMEM((2, NX - 1, ROWS, WIDTH), BF16),
+            pltpu.VMEM((NX - 1, ROWS, WIDTH), BF16),
+            pltpu.VMEM((NX - 1, ROWS, WIDTH), BF16),
+            pltpu.VMEM((6, ROWS // 2, WIDTH), BF16),
+            pltpu.VMEM((6, ROWS // 2, WIDTH), BF16),
+            pltpu.VMEM((2, ROWS // 2, WIDTH), F32),
             pltpu.VMEM((2, ROWS, WIDTH), F32),
             pltpu.VMEM((ROWS, WIDTH), BF16),
             pltpu.VMEM((ROWS, WIDTH), BF16),
-            dma((7,)), dma, dma, dma, dma((2,)), dma((CTX // TILE,)), dma, dma, dma,
-            dma((2, NX - 1, CHUNKS)), dma((2, NX - 1, CHUNKS)), dma((CHUNKS,)), dma((CHUNKS,)),
+            dma((7,)), dma, dma, dma, dma((3,)), dma((CTX // TILE,)), dma((2,)), dma((4,)), dma((4,)),
+            dma((NX - 1, CHUNKS)), dma((NX - 1, CHUNKS)), dma((6,)), dma((6,)), dma((CHUNKS,)), dma((CHUNKS,)),
         ],
         compiler_params=pltpu.CompilerParams(
             collective_id=0, has_side_effects=True, vmem_limit_bytes=56 << 20

time: 47.6 us -> 46.2 us (0.971)
  Pallas kernels: 46.8 us -> 45.4 us
    pallas_call x1, Pallas kernels: 46.8 us -> 45.4 us  [per_device(): pl.pallas_call(kernel, name='hyena', out_shape=pltpu.VMEM((ROWS, WIDTH),...]
where the time goes in v3:
time: 46.2 us; the launch traced here: 46.1 us
  Pallas kernels  45.4 us (98%)
  local copies, waits for them, and re-layouts  0.66 us (1%)
    pallas_call x1, Pallas kernels, per_device(): pl.pallas_call(kernel, name='hyena', out_shape=pltpu.VMEM((ROWS, WIDTH),...  45.4 us

profile of v3, /device:TPU:1, one launch (start us, length us, event | category | flops | bytes accessed | tf_op | source)
XLA Modules:
  0.0 46.1 jit_solution(14744932497179367257)
XLA Ops:
  0.0 45.4 %hyena.1 = bf16[256,256]{1,0:T(8,128)(2,1)S(1)} custom-call(bf16[256,256]{1,0:T(8,128)(2,1)} %gate_hbm.1, bf16[256,256]{1,0:T(8,128)(2,1)} %key_hbm.1, bf16[256,256]{1,0:T(8,128)(2,1)} %value_hbm.1, f32[256,256]{1,0:T(8,128)} %filters_hbm.1, f32[1,256]{1,0:T(1,128)} %bitcast.1, bf16[256,4096]{1,0:T(8,128)(2,1)} %weight_hbm.1, ...), custom_call_target="tpu_custom_call" | custom-call | tf_op jit(solution)/shard_map/hyena/pallas_call | solution.py:289
  45.4 0.7 %copy.10 = bf16[256,256]{1,0:T(8,128)(2,1)} copy(bf16[256,256]{1,0:T(8,128)(2,1)S(1)} %hyena.1) | data formatting | bytes 262144

commit v4 on v3

--- a/solution.py
+++ b/solution.py
@@ -19,6 +19,7 @@
 OWN = WIDTH // CTX
 NX = 4
 CHUNKS = 4
+STRIDE = 5
 TILE = 4
 
 
@@ -51,6 +52,17 @@
     def along_x(d):
         return (c, ((x + d) % NX) * 4 + yhi * 2 + core)
 
+    barrier = pltpu.get_barrier_semaphore()
+
+    def greet(k, carry):
+        pl.semaphore_signal(barrier, inc=1, device_id=((c + k) % CTX, h), device_id_type=MESH)
+        return carry
+
+    lax.fori_loop(1, CTX, greet, 0, unroll=True)
+    others = [sibling, across] + [along_x(d) for d in range(1, NX)]
+    for dev in others:
+        pl.semaphore_signal(barrier, inc=1, device_id=dev, device_id_type=MESH)
+
     loads = []
     for i, (src, dst) in enumerate(
         [(key_hbm, key.at[0]), (value_hbm, value.at[0]), (filters_hbm, filters), (fwd_hbm, fwd),
@@ -60,17 +72,6 @@
         load.start()
         loads.append(load)
 
-    barrier = pltpu.get_barrier_semaphore()
-
-    def greet(k, carry):
-        pl.semaphore_signal(barrier, inc=1, device_id=((c + k) % CTX, h), device_id_type=MESH)
-        return carry
-
-    lax.fori_loop(1, CTX, greet, 0, unroll=True)
-    others = [sibling, across] + [along_x(d) for d in range(1, NX)]
-    for dev in others:
-        pl.semaphore_signal(barrier, inc=1, device_id=dev, device_id_type=MESH)
-
     for i in range(2 * NX):
         copy = pltpu.make_async_copy(
             weight_hbm.at[:, pl.ds(pl.multiple_of((2 * i + core) * WIDTH, WIDTH), WIDTH)],
@@ -90,15 +91,12 @@
 
     pl.semaphore_wait(barrier, CTX - 1 + len(others))
 
-    def scatter1(k, carry):
-        to = (c + k) % CTX
+    for k in range(1, CTX):
+        to = (c + k * STRIDE % CTX) % CTX
         pltpu.make_async_remote_copy(
             src_ref=send1.at[to], dst_ref=recv1.at[c], send_sem=send_sem.at[0],
             recv_sem=recv_sem.at[c // TILE], device_id=(to, h), device_id_type=MESH,
         ).start()
-        return carry
-
-    lax.fori_loop(1, CTX, scatter1, 0, unroll=True)
 
     for i in range(2 * NX):
         pltpu.make_async_remote_copy(

time: 46.2 us -> 45.5 us (0.985); the launches traced: 46.1 us -> 44.8 us
  Pallas kernels: 45.4 us -> 44.1 us
    pallas_call x1, Pallas kernels: 45.4 us -> 44.1 us  [per_device(): pl.pallas_call(kernel, name='hyena', out_shape=pltpu.VMEM((ROWS, WIDTH),...]
where the time goes in v4:
time: 45.5 us; the launch traced here: 44.8 us
  Pallas kernels  44.1 us (97%)
  local copies, waits for them, and re-layouts  0.66 us (1%)
    pallas_call x1, Pallas kernels, per_device(): pl.pallas_call(kernel, name='hyena', out_shape=pltpu.VMEM((ROWS, WIDTH),...  44.1 us

profile of v4, /device:TPU:1, one launch (start us, length us, event | category | flops | bytes accessed | tf_op | source)
XLA Modules:
  0.0 44.8 jit_solution(1526610491850647307)
XLA Ops:
  0.0 44.1 %hyena.1 = bf16[256,256]{1,0:T(8,128)(2,1)S(1)} custom-call(bf16[256,256]{1,0:T(8,128)(2,1)} %gate_hbm.1, bf16[256,256]{1,0:T(8,128)(2,1)} %key_hbm.1, bf16[256,256]{1,0:T(8,128)(2,1)} %value_hbm.1, f32[256,256]{1,0:T(8,128)} %filters_hbm.1, f32[1,256]{1,0:T(1,128)} %bitcast.1, bf16[256,4096]{1,0:T(8,128)(2,1)} %weight_hbm.1, ...), custom_call_target="tpu_custom_call" | custom-call | tf_op jit(solution)/shard_map/hyena/pallas_call | solution.py:287
  44.1 0.7 %copy.10 = bf16[256,256]{1,0:T(8,128)(2,1)} copy(bf16[256,256]{1,0:T(8,128)(2,1)S(1)} %hyena.1) | data formatting | bytes 262144

commit v5 on v4

--- a/solution.py
+++ b/solution.py
@@ -18,8 +18,11 @@
 WIDTH = 256
 OWN = WIDTH // CTX
 NX = 4
-CHUNKS = 4
+SIZES = (64, 64, 64, 32)
+MAIN = sum(SIZES)
+REST = ROWS - MAIN
 STRIDE = 5
+MID = 3
 TILE = 4
 
 
@@ -37,7 +40,7 @@
     out_ref,
     gate, key, value, filters, skip, fwd, bwd,
     send1, recv1, sig, fil, send2, recv2,
-    gated, weight, part, got, ring, ringgot, onward, own, ypart, ygot,
+    gated, weight, part, got, ring, ringgot, onward, own, ypart, ygot, ahead, aheadgot, onrest,
     in_sem, w_sem, wsend_sem, wrecv_sem, send_sem, recv_sem, recv2_sem, gsend_sem, grecv_sem,
     xsend_sem, xrecv_sem, rsend_sem, rrecv_sem, ysend_sem, yrecv_sem,
 ):
@@ -208,12 +211,14 @@
         )
 
     order = (2, 1, 3)
-    step = ROWS // CHUNKS
-    half = ROWS // 2
-    top, bottom = slice(0, half), slice(half, ROWS)
+    half = MAIN // 2
+    top, bottom, rest = slice(0, half), slice(half, MAIN), slice(MAIN, ROWS)
+
+    def chunk(r):
+        return pl.ds(sum(SIZES[:r]), SIZES[r])
 
     def send_across(r):
-        rows = pl.ds(step * r, step)
+        rows = chunk(r)
         copies = []
         for k, d in enumerate(order):
             part[k, rows] = block(d, 1 - yhi, rows).astype(BF16)
@@ -238,7 +243,14 @@
         ringcopies[i].wait_recv()
         return ringgot[i].astype(F32)
 
-    first = [send_across(r) for r in range(CHUNKS)]
+    for d in range(NX):
+        ahead[d] = block(d, 1 - yhi, rest).astype(BF16)
+    aheadcopy = pltpu.make_async_remote_copy(
+        src_ref=ahead, dst_ref=aheadgot, send_sem=ysend_sem.at[len(SIZES)],
+        recv_sem=yrecv_sem.at[len(SIZES)], device_id=across, device_id_type=MESH,
+    )
+    aheadcopy.start()
+    first = [send_across(r) for r in range(len(SIZES))]
     far = block(2, yhi)
     ringcopies = [send_ring(0, far[top]), send_ring(1, far[bottom])]
     right, left = block(1, yhi), block(3, yhi)
@@ -246,10 +258,28 @@
     onward[0] = right[top]
     onward[1] = left[bottom]
     own[0] = block(0, 1 - yhi)
+    for d, terms in ((1, right), (2, far), (3, left)):
+        onrest[d - 1] = terms[rest]
     own[1] = block(0, yhi)
-    ycopies = []
-    for r in range(CHUNKS):
-        rows = pl.ds(step * r, step)
+    ycopies = [aheadcopy]
+    restcopies = []
+
+    def send_rest():
+        aheadcopy.wait_recv()
+        for k, d in enumerate(order):
+            part[k, rest] = (onrest[d - 1] + aheadgot[d].astype(F32)).astype(BF16)
+            copy = pltpu.make_async_remote_copy(
+                src_ref=part.at[k, pl.ds(MAIN, REST)], dst_ref=got.at[k, pl.ds(MAIN, REST)],
+                send_sem=xsend_sem.at[k, len(SIZES)], recv_sem=xrecv_sem.at[k, len(SIZES)],
+                device_id=along_x(d), device_id_type=MESH,
+            )
+            copy.start()
+            restcopies.append(copy)
+
+    for r in range(len(SIZES)):
+        if r == MID:
+            send_rest()
+        rows = chunk(r)
         total = own[0, rows]
         for k in range(NX - 1):
             first[r][k].wait_recv()
@@ -264,9 +294,14 @@
     ringcopies += [send_ring(4 + i, onward[i] + arrived(i)) for i in range(2)]
     own[1, top] = own[1, top] + arrived(3) + arrived(4)
     own[1, bottom] = own[1, bottom] + arrived(2) + arrived(5)
-    for r in range(CHUNKS):
-        rows = pl.ds(step * r, step)
-        ycopies[r].wait_recv()
+    total = own[1, rest] + aheadgot[0].astype(F32)
+    for k in range(NX - 1):
+        restcopies[k].wait_recv()
+        total = total + got[k, rest].astype(F32)
+    out_ref[rest] = total.astype(BF16)
+    for r in range(len(SIZES)):
+        rows = chunk(r)
+        ycopies[r + 1].wait_recv()
         out_ref[rows] = (own[1, rows] + ygot[rows].astype(F32)).astype(BF16)
 
     for n, count in enumerate((CTX - 1, CTX - 1, CTX)):
@@ -276,7 +311,7 @@
             device_id=sibling, device_id_type=MESH,
         ).wait_send()
     waitw.wait_send()
-    for copy in streams + sum(first, []) + ringcopies + ycopies:
+    for copy in streams + sum(first, []) + ringcopies + ycopies + restcopies:
         copy.wait_send()
 
 
@@ -308,14 +343,17 @@
             pltpu.VMEM((2 * NX, 2 * WIDTH, WIDTH), BF16),
             pltpu.VMEM((NX - 1, ROWS, WIDTH), BF16),
             pltpu.VMEM((NX - 1, ROWS, WIDTH), BF16),
-            pltpu.VMEM((6, ROWS // 2, WIDTH), BF16),
-            pltpu.VMEM((6, ROWS // 2, WIDTH), BF16),
-            pltpu.VMEM((2, ROWS // 2, WIDTH), F32),
+            pltpu.VMEM((6, MAIN // 2, WIDTH), BF16),
+            pltpu.VMEM((6, MAIN // 2, WIDTH), BF16),
+            pltpu.VMEM((2, MAIN // 2, WIDTH), F32),
             pltpu.VMEM((2, ROWS, WIDTH), F32),
             pltpu.VMEM((ROWS, WIDTH), BF16),
             pltpu.VMEM((ROWS, WIDTH), BF16),
+            pltpu.VMEM((NX, REST, WIDTH), BF16),
+            pltpu.VMEM((NX, REST, WIDTH), BF16),
+            pltpu.VMEM((NX - 1, REST, WIDTH), F32),
             dma((7,)), dma, dma, dma, dma((3,)), dma((CTX // TILE,)), dma((2,)), dma((4,)), dma((4,)),
-            dma((NX - 1, CHUNKS)), dma((NX - 1, CHUNKS)), dma((6,)), dma((6,)), dma((CHUNKS,)), dma((CHUNKS,)),
+            dma((NX - 1, len(SIZES) + 1)), dma((NX - 1, len(SIZES) + 1)), dma((6,)), dma((6,)), dma((len(SIZES) + 1,)), dma((len(SIZES) + 1,)),
         ],
         compiler_params=pltpu.CompilerParams(
             collective_id=0, has_side_effects=True, vmem_limit_bytes=56 << 20

time: 45.5 us -> 45.5 us (level); the launches traced: 44.8 us -> 45.3 us
  Pallas kernels: 44.1 us -> 44.7 us
    pallas_call x1, Pallas kernels: 44.1 us -> 44.7 us  [per_device(): pl.pallas_call(kernel, name='hyena', out_shape=pltpu.VMEM((ROWS, WIDTH),...]
where the time goes in v5:
time: 45.5 us; the launch traced here: 45.3 us
  Pallas kernels  44.7 us (98%)
  local copies, waits for them, and re-layouts  0.66 us (1%)
    pallas_call x1, Pallas kernels, per_device(): pl.pallas_call(kernel, name='hyena', out_shape=pltpu.VMEM((ROWS, WIDTH),...  44.7 us

profile of v5, /device:TPU:1, one launch (start us, length us, event | category | flops | bytes accessed | tf_op | source)
XLA Modules:
  0.0 45.3 jit_solution(10796308726383971529)
XLA Ops:
  0.0 44.7 %hyena.1 = bf16[256,256]{1,0:T(8,128)(2,1)S(1)} custom-call(bf16[256,256]{1,0:T(8,128)(2,1)} %gate_hbm.1, bf16[256,256]{1,0:T(8,128)(2,1)} %key_hbm.1, bf16[256,256]{1,0:T(8,128)(2,1)} %value_hbm.1, f32[256,256]{1,0:T(8,128)} %filters_hbm.1, f32[1,256]{1,0:T(1,128)} %bitcast.1, bf16[256,4096]{1,0:T(8,128)(2,1)} %weight_hbm.1, ...), custom_call_target="tpu_custom_call" | custom-call | tf_op jit(solution)/shard_map/hyena/pallas_call | solution.py:322
  44.7 0.7 %copy.10 = bf16[256,256]{1,0:T(8,128)(2,1)} copy(bf16[256,256]{1,0:T(8,128)(2,1)S(1)} %hyena.1) | data formatting | bytes 262144
